TPU v7x, 128 devices: a whole 4x4x4 slice. The times are simulated.
128 devices in a mesh: ctx: 16 (over x, y_lo, core), head: 8 (over y_hi, z).
Axes of the slice: x: 4, y: 4 (y_hi: 2, y_lo: 2; y = y_hi * 2 + y_lo), z: 4, core: 2. Of those that a mesh axis runs over, the one named last changes fastest.
Arguments:
- q_nope: bfloat16 [4096, 4096], P('ctx', 'head'), may hold values from -5 to 5
- q_rope: bfloat16 [4096, 2048], P('ctx', 'head'), may hold values from -320 to 320
- latent: bfloat16 [4096, 512], P('ctx'), may hold values from -5 to 5
- rope_keys: bfloat16 [4096, 64], P('ctx'), may hold values from -4.5 to 4.5
- out_grad: bfloat16 [4096, 4096], P('ctx', 'head'), may hold values from -96 to 96
- up_keys: bfloat16 [512, 4096], P(None, 'head'), may hold values from -0.25 to 0.25
- up_values: bfloat16 [512, 4096], P(None, 'head'), may hold values from -0.25 to 0.25
- group_order: int32 [32], replicated, may hold values from 0 to 31, each once
Outputs:
- grad_q_nope: bfloat16 [4096, 4096], P('ctx', 'head')
- grad_q_rope: bfloat16 [4096, 2048], P('ctx', 'head')
- grad_latent: float32 [4096, 512], P('ctx')
- grad_rope: float32 [4096, 64], P('ctx')
- grad_up_keys: float32 [512, 4096], P('ctx', 'head')
- grad_up_values: float32 [512, 4096], P('ctx', 'head')
Inputs may be any that keep to these rules, and one draw needn't show every extreme that they name: `group_order`: each group place appears once.
All inputs are finite; a program needn't handle non-finite values.
Results may differ from a plain program's by a relative error of at most 0.0087.
Values may be sent and summed in bfloat16 or wider, within the bound.
A program may use at most 128 MiB of HBM per device.

v0:
```python
import math
import jax
import jax.numpy as jnp
from jax import lax
from jax.sharding import PartitionSpec as P

ROPE = 64
HEAD_DIM = 128
H_DEV = 4
GROUP = 128
NEG_LARGE = -1e30


def positions(group_order, first_row, count):
    rows = first_row + jnp.arange(count, dtype=jnp.int32)
    group_ids = rows // GROUP
    table = jnp.arange(group_order.shape[0], dtype=jnp.int32)
    placed = jnp.sum(
        jnp.where(group_ids[:, None] == table[None, :], group_order[None, :], 0), axis=1
    )
    return placed * GROUP + rows % GROUP


def per_device(q_nope, q_rope, latent, rope_keys, out_grad, up_keys, up_values, group_order):
    width = q_nope.shape[0]
    scale = (HEAD_DIM + ROPE) ** (-0.5)
    seq_len = lax.axis_size("ctx") * width
    q_pos = positions(group_order, lax.axis_index("ctx") * width, width)
    query_nope = q_nope.reshape(width, H_DEV, HEAD_DIM)
    query_rope = q_rope.reshape(width, H_DEV, ROPE)
    grad_heads = out_grad.reshape(width, H_DEV, HEAD_DIM)
    pair_cols = 2 * H_DEV * HEAD_DIM
    latent_all, rope_all = (
        lax.all_gather(latent, "ctx", axis=0, tiled=True),
        lax.all_gather(rope_keys, "ctx", axis=0, tiled=True),
    )
    keys_all = jnp.dot(latent_all, up_keys, preferred_element_type=jnp.float32).astype(jnp.bfloat16)
    values_all = jnp.dot(latent_all, up_values, preferred_element_type=jnp.float32).astype(
        jnp.bfloat16
    )

    def fetch(start, count):
        key_rows = lax.dynamic_slice_in_dim(keys_all, start, count, 0).reshape(
            count, H_DEV, HEAD_DIM
        )
        value_rows = lax.dynamic_slice_in_dim(values_all, start, count, 0).reshape(
            count, H_DEV, HEAD_DIM
        )
        rope_rows = lax.dynamic_slice_in_dim(rope_all, start, count, 0)
        return (key_rows, value_rows, rope_rows)

    def block_scores(key_rows, rope_rows, k_pos):
        raw = jnp.einsum("thd,khd->htk", query_nope, key_rows, preferred_element_type=jnp.float32)
        raw = raw + jnp.einsum(
            "thr,kr->htk", query_rope, rope_rows, preferred_element_type=jnp.float32
        )
        visible = (k_pos[None, :] <= q_pos[:, None])[None]
        return (jnp.where(visible, raw * scale, NEG_LARGE), visible)

    block = math.gcd(seq_len, 512)
    block_count = seq_len // block

    def stats_visit(carry, index):
        start = index * block
        k_pos = positions(group_order, start, block)
        row_top, row_total, weighted = carry
        key_rows, value_rows, rope_rows = fetch(start, block)
        score, visible = block_scores(key_rows, rope_rows, k_pos)
        dattn = jnp.einsum(
            "thd,khd->htk", grad_heads, value_rows, preferred_element_type=jnp.float32
        )
        new_top = jnp.maximum(row_top, jnp.max(score, axis=2))
        factor = jnp.exp(row_top - new_top)
        expd = jnp.where(visible, jnp.exp(score - new_top[..., None]), 0.0)
        new_total = row_total * factor + jnp.sum(expd, axis=2)
        new_weighted = weighted * factor + jnp.sum(expd * dattn, axis=2)
        carry = (new_top, new_total, new_weighted)
        return (carry, None)

    start_top = jnp.full((H_DEV, width), NEG_LARGE, jnp.float32)
    zeros_rows = jnp.zeros((H_DEV, width), jnp.float32)
    row_top, row_total, weighted = lax.scan(
        stats_visit, (start_top, zeros_rows, zeros_rows), jnp.arange(block_count, dtype=jnp.int32)
    )[0]
    delta = weighted / row_total

    def grad_visit(carry, index):
        start = index * block
        k_pos = positions(group_order, start, block)
        acc_nope, acc_rope = carry
        key_rows, value_rows, rope_rows = fetch(start, block)
        score, visible = block_scores(key_rows, rope_rows, k_pos)
        attn = jnp.where(visible, jnp.exp(score - row_top[..., None]) / row_total[..., None], 0.0)
        dattn = jnp.einsum(
            "thd,khd->htk", grad_heads, value_rows, preferred_element_type=jnp.float32
        )
        dscore = (attn * (dattn - delta[..., None])).astype(jnp.bfloat16)
        acc_nope = acc_nope + jnp.einsum(
            "htk,khd->thd", dscore, key_rows, preferred_element_type=jnp.float32
        )
        acc_rope = acc_rope + jnp.einsum(
            "htk,kr->thr", dscore, rope_rows, preferred_element_type=jnp.float32
        )
        dkey = (
            jnp.einsum("htk,thd->khd", dscore, query_nope, preferred_element_type=jnp.float32)
            * scale
        )
        dvalue = jnp.einsum(
            "htk,thd->khd",
            attn.astype(jnp.bfloat16),
            grad_heads,
            preferred_element_type=jnp.float32,
        )
        drope = (
            jnp.einsum("htk,thr->kr", dscore, query_rope, preferred_element_type=jnp.float32)
            * scale
        )
        pair_terms = jnp.stack([dkey, dvalue], axis=1).reshape(block, pair_cols)
        return ((acc_nope, acc_rope), (pair_terms, drope))

    start_nope = jnp.zeros((width, H_DEV, HEAD_DIM), jnp.float32)
    start_rope = jnp.zeros((width, H_DEV, ROPE), jnp.float32)
    (acc_nope, acc_rope), (pair_stack, rope_stack) = lax.scan(
        grad_visit, (start_nope, start_rope), jnp.arange(block_count, dtype=jnp.int32)
    )
    grad_q_nope = (acc_nope * scale).astype(jnp.bfloat16).reshape(width, H_DEV * HEAD_DIM)
    grad_q_rope = (acc_rope * scale).astype(jnp.bfloat16).reshape(width, H_DEV * ROPE)
    pair_sum, rope_part = (
        lax.psum_scatter(
            pair_stack.reshape(seq_len, pair_cols), "ctx", scatter_dimension=0, tiled=True
        ),
        lax.psum_scatter(rope_stack.reshape(seq_len, ROPE), "ctx", scatter_dimension=0, tiled=True),
    )
    pair_sum = pair_sum.reshape(width, 2, H_DEV * HEAD_DIM)
    dkeys = pair_sum[:, 0].astype(jnp.bfloat16)
    dvalues = pair_sum[:, 1].astype(jnp.bfloat16)
    contract_cols = (((1,), (1,)), ((), ()))
    latent_part = lax.dot_general(dkeys, up_keys, contract_cols, preferred_element_type=jnp.float32)
    latent_part = latent_part + lax.dot_general(
        dvalues, up_values, contract_cols, preferred_element_type=jnp.float32
    )
    grad_latent, grad_rope = lax.psum((latent_part, rope_part), "head")
    contract_rows = (((0,), (0,)), ((), ()))
    weight_keys = lax.dot_general(latent, dkeys, contract_rows, preferred_element_type=jnp.float32)
    weight_values = lax.dot_general(
        latent, dvalues, contract_rows, preferred_element_type=jnp.float32
    )
    grad_up_keys, grad_up_values = (
        lax.psum_scatter(weight_keys, "ctx", scatter_dimension=0, tiled=True),
        lax.psum_scatter(weight_values, "ctx", scatter_dimension=0, tiled=True),
    )
    return (grad_q_nope, grad_q_rope, grad_latent, grad_rope, grad_up_keys, grad_up_values)


def solution(mesh):
    in_specs = (
        P("ctx", "head"),
        P("ctx", "head"),
        P("ctx", None),
        P("ctx", None),
        P("ctx", "head"),
        P(None, "head"),
        P(None, "head"),
        P(),
    )
    out_specs = (
        P("ctx", "head"),
        P("ctx", "head"),
        P("ctx", None),
        P("ctx", None),
        P("ctx", "head"),
        P("ctx", "head"),
    )
    return jax.shard_map(
        per_device, mesh=mesh, in_specs=in_specs, out_specs=out_specs, check_vma=False
    )
```

profile of v0, /device:TPU:0, one launch (start us, length us, event | category | flops | bytes accessed | tf_op | source)
XLA Modules:
  0.0 750.5 jit_solution(6171262483542442688)
XLA Ops:
  11.8 22.9 %all_gather.7 = bf16[4096,64]{0,1:T(8,128)(2,1)} all-gather(bf16[256,64]{0,1:T(8,128)(2,1)S(1)} %copy-done.6), channel_id=1, replica_groups=mesh['ctx'=16,'head'=8] {'ctx'}, dimensions={0}, use_global_device_ids=true | all-gather | bytes 557056 | tf_op jit(solution)/shard_map/all_gather | solution.py:35
  34.7 15.2 %all-gather.2.cloned.1.call-done = bf16[4096,512]{1,0:T(8,128)(2,1)} async-done(((bf16[256,512]{1,0:T(8,128)(2,1)}), bf16[4096,512]{1,0:T(8,128)(2,1)}) %all-gather.2.cloned.1.call-update) | async-done | bytes 4194320 | tf_op jit(solution)/shard_map/all_gather | solution.py:34
  49.9 6.5 convolution_convert_fusion
  56.4 6.4 copy.104
  62.7 6.5 convolution_convert_fusion.1
  69.2 6.4 copy.106
  75.6 47.8 %while.36 = (s32[]{:T(128)}, f32[4,256]{1,0:T(4,128)S(1)}, f32[4,256]{1,0:T(4,128)S(1)}, f32[4,256]{1,0:T(4,128)S(1)}, s32[8]{0:T(128)S(1)}, /*index=5*/s32[32]{...) while((s32[]{:T(128)}, f32[4,256]{1,0:T(4,128)S(1)}, ...), condition=%wide.region_6.7_spmd.clone, body=%wide.region_1.6_spmd.clone.sunk | while | flops 341513728 | bytes 14964090 | solution.py:82
  123.5 158.1 %while.37 = (s32[]{:T(128)}, f32[256,4,128]{0,2,1:T(8,128)}, f32[256,4,64]{0,2,1:T(8,128)}, f32[8,512,1024]{2,1,0:T(8,128)}, f32[8,512,64]{1,0,2:T(8,128)}, /*in...) while((s32[]{:T(128)}, f32[256,4,128]{0,2,1:T(8,128)}, ...), condition=%wide.region_9.10_spmd.clone, body=%wide.region_7.9_spmd.clone.sunk | while | flops 879065600 | bytes 38036900 | solution.py:123
  126.8 1.7 fusion.133
  131.2 1.9 fusion.136
  133.5 1.5 pad_maximum_fusion.2
  135.1 1.9 copy.147
  137.0 3.8 dynamic_update_slice.20
  140.7 1.5 constant_dynamic-update-slice_fusion.2
  145.5 1.7 fusion.133
  148.2 2.2 fusion.135
  151.0 2.0 fusion.136
  153.4 1.5 pad_maximum_fusion.2
  155.0 1.9 copy.147
  156.9 3.8 dynamic_update_slice.20
  165.4 1.7 fusion.133
  168.1 2.2 fusion.135
  170.8 2.0 fusion.136
  173.3 1.5 pad_maximum_fusion.2
  174.9 1.9 copy.147
  176.8 3.8 dynamic_update_slice.20
  185.3 1.7 fusion.133
  188.0 2.2 fusion.135
  190.8 2.0 fusion.136
  193.2 1.5 pad_maximum_fusion.2
  194.8 1.9 copy.147
  196.7 3.8 dynamic_update_slice.20
  205.2 1.7 fusion.133
  207.9 2.2 fusion.135
  210.7 2.0 fusion.136
  213.2 1.5 pad_maximum_fusion.2
  214.7 1.9 copy.147
  216.6 3.8 dynamic_update_slice.20
  220.4 1.5 constant_dynamic-update-slice_fusion.2
  225.2 1.7 fusion.133
  227.9 2.2 fusion.135
  230.6 2.0 fusion.136
  233.1 1.5 pad_maximum_fusion.2
  234.7 1.9 copy.147
  236.6 3.8 dynamic_update_slice.20
  245.1 1.7 fusion.133
  247.8 2.2 fusion.135
  250.5 2.0 fusion.136
  253.0 1.5 pad_maximum_fusion.2
  254.6 1.9 copy.147
  256.5 3.8 dynamic_update_slice.20
  265.0 1.7 fusion.133
  267.7 2.2 fusion.135
  270.4 2.0 fusion.136
  272.9 1.5 pad_maximum_fusion.2
  274.5 1.9 copy.147
  276.4 3.8 dynamic_update_slice.20
  282.8 1.6 copy.138
  284.5 174.1 %reduce-scatter.9.cloned.1.call-done = f32[256,1024]{1,0:T(8,128)} async-done(((f32[4096,1024]{1,0:T(8,128)}), f32[256,1024]{1,0:T(8,128)}) %reduce-scatter.9.cloned.1.call-update) | async-done | bytes 1048592 | tf_op jit(solution)/shard_map/reduce_scatter | solution.py:129
  462.5 65.2 %reduce-scatter.11.cloned.1.call-done = f32[256,64]{0,1:T(8,128)} async-done(((f32[4096,64]{0,1:T(8,128)}), f32[256,64]{0,1:T(8,128)}) %reduce-scatter.11.cloned.1.call-update) | async-done | bytes 65552 | tf_op jit(solution)/shard_map/reduce_scatter | solution.py:132
  535.0 80.0 %all-reduce.3.cloned.1.call-done = (f32[256,512]{1,0:T(8,128)}, f32[256,64]{0,1:T(8,128)}) async-done(((f32[256,512]{1,0:T(8,128)}, f32[256,64]{0,1:T(8,128)}), (f32[256,512]{1,0:T(8,128)}, f32[256,64]{0,1:T(8,128)})) %all-reduce.3.cloned.1.call-update) | async-done | bytes 589840 | tf_op jit(solution)/shard_map/psum | solution.py:142
  615.0 62.4 %reduce-scatter.15.cloned.1.call-done = f32[32,512]{1,0:T(8,128)} async-done(((f32[512,512]{1,0:T(8,128)}), f32[32,512]{1,0:T(8,128)}) %reduce-scatter.15.cloned.1.call-update) | async-done | bytes 65552
  677.4 62.9 %reduce-scatter.13.cloned.1.call-done = f32[32,512]{1,0:T(8,128)} async-done(((f32[512,512]{1,0:T(8,128)}), f32[32,512]{1,0:T(8,128)}) %reduce-scatter.13.cloned.1.call-update) | async-done | bytes 65552
  740.3 1.9 copy.180
  (265 shorter events, 107.1 us)
Async XLA Ops:
  7.2 55.6 %copy-start = (bf16[512,512]{1,0:T(8,128)(2,1)S(1)}, bf16[512,512]{1,0:T(8,128)(2,1)}, u32[]{:S(2)}) copy-start(bf16[512,512]{1,0:T(8,128)(2,1)} %param.17) | copy-start | bytes 1572868
  7.2 4.5 copy-start.5
  7.2 4.6 copy-start.6
  7.2 42.7 %copy-start.3 = (bf16[512,512]{1,0:T(8,128)(2,1)S(1)}, bf16[512,512]{1,0:T(8,128)(2,1)}, u32[]{:S(2)}) copy-start(bf16[512,512]{1,0:T(8,128)(2,1)} %param.18) | copy-start | bytes 1572868
  7.2 42.7 %all-gather.2.cloned.1.call-start = ((), (), s32[]{:S(2)}) async-start(), calls=%async_computation.4 | async-start | bytes 4456448 | tf_op jit(solution)/shard_map/all_gather | solution.py:34
  7.9 450.6 %reduce-scatter.9.cloned.1.call-start = ((), (), s32[]{:S(2)}) async-start(), calls=%async_computation.5 | async-start | bytes 17825792 | tf_op jit(solution)/shard_map/reduce_scatter | solution.py:129
  281.6 1.2 copy-start.2
  281.6 246.1 %reduce-scatter.11.cloned.1.call-start = ((), (), s32[]{:S(2)}) async-start(), calls=%async_computation.6 | async-start | bytes 1114112 | tf_op jit(solution)/shard_map/reduce_scatter | solution.py:132
  284.5 330.5 %all-reduce.3.cloned.1.call-start = ((), (), s32[]{:S(2)}) async-start(), calls=%async_computation.9 | async-start | bytes 1179648 | tf_op jit(solution)/shard_map/psum | solution.py:142
  459.9 1.5 copy-start.4
  461.0 66.8 %copy-start.1 = (bf16[256,512]{1,0:T(8,128)(2,1)S(1)}, bf16[256,512]{1,0:T(8,128)(2,1)}, u32[]{:S(2)}) copy-start(bf16[256,512]{1,0:T(8,128)(2,1)} %param.14) | copy-start | bytes 786436
  527.8 149.6 %reduce-scatter.15.cloned.1.call-start = ((), (), s32[]{:S(2)}) async-start(), calls=%async_computation.8 | async-start | bytes 1114112
  529.6 210.8 %reduce-scatter.13.cloned.1.call-start = ((), (), s32[]{:S(2)}) async-start(), calls=%async_computation.7 | async-start | bytes 1114112
Sparse Core Ops, SparseCore 0:
  9.8 40.0 all-gather.1
  281.8 176.7 reduce-scatter.8
  461.0 66.7 reduce-scatter.10
  530.3 84.6 all-reduce.2
  617.9 59.4 reduce-scatter.14
  680.2 60.1 reduce-scatter.12
where the time goes:
time: 754 us; the launch traced here: 751 us
  waiting for transfers between devices  461 us (61%)
  local copies, waits for them, and re-layouts  116 us (15%)
  matrix products  102 us (14%)
  other arithmetic  23.3 us (3%)
  blocking collectives  22.9 us (3%)
  between operations  14.4 us (2%)
  loops' own time  11.6 us (2%)
    reduce_scatter x1, waiting for transfers between devices, per_device(): lax.psum_scatter(pair_stack.reshape(seq_len, pair_cols), 'ctx', scatter_d...  174 us
    unnamed x8, waiting for transfers between devices  126 us
    psum x1, waiting for transfers between devices, per_device(): grad_latent, grad_rope = lax.psum((latent_part, rope_part), 'head')  80 us
    reduce_scatter x1, waiting for transfers between devices, per_device(): lax.psum_scatter(rope_stack.reshape(seq_len, ROPE), 'ctx', scatter_dimens...  65.2 us
    dynamic_update_slice x32, local copies, waits for them, and re-layouts, per_device(): lax.scan(grad_visit, (start_nope, start_rope), jnp.arange(block_count, dt...  58.2 us
    unnamed x27, local copies, waits for them, and re-layouts  25.7 us
    dot_general x16, matrix products, block_scores(): jnp.einsum('thr,kr->htk', query_rope, rope_rows, preferred_element_type=j...  25.4 us
    all_gather x1, blocking collectives, per_device(): lax.all_gather(rope_keys, 'ctx', axis=0, tiled=True)  22.9 us
  transfers between devices with their start and end apart: 6, of which 6 were waited for; matrix products, arithmetic and copies ran while one was open for 2% of the time, Pallas kernels for 0%

commit v1 on v0

--- a/solution.py
+++ b/solution.py
@@ -31,7 +31,9 @@
     grad_heads = out_grad.reshape(width, H_DEV, HEAD_DIM)
     pair_cols = 2 * H_DEV * HEAD_DIM
     latent_all, rope_all = (
-        lax.all_gather(latent, "ctx", axis=0, tiled=True),
+        jnp.concatenate(
+            lax.all_to_all(jnp.stack([latent] * lax.axis_size("ctx")), "ctx", 0, 0), axis=0
+        ),
         lax.all_gather(rope_keys, "ctx", axis=0, tiled=True),
     )
     keys_all = jnp.dot(latent_all, up_keys, preferred_element_type=jnp.float32).astype(jnp.bfloat16)

time: 754 us -> 794 us (1.053)
  blocking collectives: 22.9 us -> 73.1 us
  waiting for transfers between devices: 461 us -> 444 us
    all_gather x1, blocking collectives: 22.9 us -> 73.1 us  [per_device(): lax.all_gather(rope_keys, 'ctx', axis=0, tiled=True)]
    all_gather x1 -> x0, waiting for transfers between devices: 15.2 us -> none  [per_device(): lax.all_gather(latent, 'ctx', axis=0, tiled=True)]
    unnamed x27 -> x33, local copies, waits for them, and re-layouts: 25.7 us -> 23.1 us
    unnamed x8 -> x7, waiting for transfers between devices: 126 us -> 125 us
  transfers between devices with their start and end apart: 6 -> 6, of which waited for: 6 -> 5; matrix products, arithmetic and copies ran while one was open for 2% -> 2% of each run, Pallas kernels for 0% -> 0%
where the time goes in v1:
time: 794 us; the launch traced here: 790 us
  waiting for transfers between devices  444 us (56%)
  local copies, waits for them, and re-layouts  116 us (15%)
  matrix products  102 us (13%)
  blocking collectives  73.1 us (9%)
  other arithmetic  23.2 us (3%)
  between operations  14.1 us (2%)
  loops' own time  11.6 us (1%)
    reduce_scatter x1, waiting for transfers between devices, per_device(): lax.psum_scatter(pair_stack.reshape(seq_len, pair_cols), 'ctx', scatter_d...  174 us
    unnamed x7, waiting for transfers between devices  125 us
    psum x1, waiting for transfers between devices, per_device(): grad_latent, grad_rope = lax.psum((latent_part, rope_part), 'head')  80.4 us
    all_gather x1, blocking collectives, per_device(): lax.all_gather(rope_keys, 'ctx', axis=0, tiled=True)  73.1 us
    reduce_scatter x1, waiting for transfers between devices, per_device(): lax.psum_scatter(rope_stack.reshape(seq_len, ROPE), 'ctx', scatter_dimens...  64.6 us
    dynamic_update_slice x32, local copies, waits for them, and re-layouts, per_device(): lax.scan(grad_visit, (start_nope, start_rope), jnp.arange(block_count, dt...  58.2 us
    dot_general x16, matrix products, block_scores(): jnp.einsum('thr,kr->htk', query_rope, rope_rows, preferred_element_type=j...  25.4 us
    unnamed x33, local copies, waits for them, and re-layouts  23.1 us
  transfers between devices with their start and end apart: 6, of which 5 were waited for; matrix products, arithmetic and copies ran while one was open for 2% of the time, Pallas kernels for 0%

profile of v1, /device:TPU:0, one launch (start us, length us, event | category | flops | bytes accessed | tf_op | source)
XLA Modules:
  0.0 790.4 jit_solution(812736082041090265)
XLA Ops:
  7.2 3.4 stack.17
  10.5 5.7 all-to-all-start
  17.3 73.1 %all_gather.3 = bf16[4096,64]{0,1:T(8,128)(2,1)} all-gather(bf16[256,64]{0,1:T(8,128)(2,1)S(1)} %copy-done.9), channel_id=1, replica_groups=mesh['ctx'=16,'head'=8] {'ctx'}, dimensions={0}, use_global_device_ids=true | all-gather | bytes 557056 | tf_op jit(solution)/shard_map/all_gather | solution.py:37
  90.4 6.5 convolution_convert_fusion
  96.9 6.4 copy.104
  103.3 6.5 convolution_convert_fusion.1
  109.8 6.4 copy.106
  116.2 47.9 %while.36 = (s32[]{:T(128)}, f32[4,256]{1,0:T(4,128)S(1)}, f32[4,256]{1,0:T(4,128)S(1)}, f32[4,256]{1,0:T(4,128)S(1)}, s32[8]{0:T(128)S(1)}, /*index=5*/s32[32]{...) while((s32[]{:T(128)}, f32[4,256]{1,0:T(4,128)S(1)}, ...), condition=%wide.region_6.7_spmd.clone, body=%wide.region_1.6_spmd.clone.sunk | while | flops 341513728 | bytes 14964090 | solution.py:84
  164.1 158.0 %while.37 = (s32[]{:T(128)}, f32[256,4,128]{0,2,1:T(8,128)}, f32[256,4,64]{0,2,1:T(8,128)}, f32[8,512,1024]{2,1,0:T(8,128)}, f32[8,512,64]{1,0,2:T(8,128)}, /*in...) while((s32[]{:T(128)}, f32[256,4,128]{0,2,1:T(8,128)}, ...), condition=%wide.region_9.10_spmd.clone, body=%wide.region_7.9_spmd.clone.sunk | while | flops 879065600 | bytes 38036900 | solution.py:125
  167.4 1.7 fusion.133
  171.8 1.9 fusion.136
  174.1 1.5 pad_maximum_fusion.2
  175.7 1.9 copy.147
  177.6 3.8 dynamic_update_slice.20
  186.1 1.7 fusion.133
  188.8 2.2 fusion.135
  191.6 2.0 fusion.136
  194.0 1.5 pad_maximum_fusion.2
  195.6 1.9 copy.147
  197.5 3.8 dynamic_update_slice.20
  206.0 1.7 fusion.133
  208.7 2.2 fusion.135
  211.4 2.0 fusion.136
  213.9 1.5 pad_maximum_fusion.2
  215.5 1.9 copy.147
  217.4 3.8 dynamic_update_slice.20
  225.9 1.7 fusion.133
  228.6 2.2 fusion.135
  231.3 2.0 fusion.136
  233.8 1.5 pad_maximum_fusion.2
  235.3 1.9 copy.147
  237.3 3.8 dynamic_update_slice.20
  245.8 1.7 fusion.133
  248.5 2.2 fusion.135
  251.2 2.0 fusion.136
  253.7 1.5 pad_maximum_fusion.2
  255.2 1.9 copy.147
  257.2 3.8 dynamic_update_slice.20
  260.9 1.5 constant_dynamic-update-slice_fusion.2
  265.7 1.7 fusion.133
  268.4 2.2 fusion.135
  271.2 2.0 fusion.136
  273.7 1.5 pad_maximum_fusion.2
  275.2 1.9 copy.147
  277.1 3.8 dynamic_update_slice.20
  285.6 1.7 fusion.133
  288.3 2.2 fusion.135
  291.1 2.0 fusion.136
  293.5 1.5 pad_maximum_fusion.2
  295.1 1.9 copy.147
  297.0 3.8 dynamic_update_slice.20
  305.5 1.7 fusion.133
  308.2 2.2 fusion.135
  311.0 2.0 fusion.136
  313.4 1.5 pad_maximum_fusion.2
  315.0 1.9 copy.147
  316.9 3.8 dynamic_update_slice.20
  323.3 1.6 copy.138
  325.2 173.9 %reduce-scatter.9.cloned.1.call-done = f32[256,1024]{1,0:T(8,128)} async-done(((f32[4096,1024]{1,0:T(8,128)}), f32[256,1024]{1,0:T(8,128)}) %reduce-scatter.9.cloned.1.call-update) | async-done | bytes 1048592 | tf_op jit(solution)/shard_map/reduce_scatter | solution.py:131
  503.1 64.6 %reduce-scatter.11.cloned.1.call-done = f32[256,64]{0,1:T(8,128)} async-done(((f32[4096,64]{0,1:T(8,128)}), f32[256,64]{0,1:T(8,128)}) %reduce-scatter.11.cloned.1.call-update) | async-done | bytes 65552 | tf_op jit(solution)/shard_map/reduce_scatter | solution.py:134
  574.8 80.4 %all-reduce.3.cloned.1.call-done = (f32[256,512]{1,0:T(8,128)}, f32[256,64]{0,1:T(8,128)}) async-done(((f32[256,512]{1,0:T(8,128)}, f32[256,64]{0,1:T(8,128)}), (f32[256,512]{1,0:T(8,128)}, f32[256,64]{0,1:T(8,128)})) %all-reduce.3.cloned.1.call-update) | async-done | bytes 589840 | tf_op jit(solution)/shard_map/psum | solution.py:144
  655.2 62.4 %reduce-scatter.15.cloned.1.call-done = f32[32,512]{1,0:T(8,128)} async-done(((f32[512,512]{1,0:T(8,128)}), f32[32,512]{1,0:T(8,128)}) %reduce-scatter.15.cloned.1.call-update) | async-done | bytes 65552
  717.6 62.9 %reduce-scatter.13.cloned.1.call-done = f32[32,512]{1,0:T(8,128)} async-done(((f32[512,512]{1,0:T(8,128)}), f32[32,512]{1,0:T(8,128)}) %reduce-scatter.13.cloned.1.call-update) | async-done | bytes 65552
  780.5 1.9 copy.180
  (271 shorter events, 105.3 us)
Async XLA Ops:
  7.2 96.1 %copy-start = (bf16[512,512]{1,0:T(8,128)(2,1)S(1)}, bf16[512,512]{1,0:T(8,128)(2,1)}, u32[]{:S(2)}) copy-start(bf16[512,512]{1,0:T(8,128)(2,1)} %param.17) | copy-start | bytes 1572868
  10.5 5.9 copy-start.7
  10.5 6.0 copy-start.5
  10.5 6.3 copy-start.6
  10.5 79.9 %all-to-all-start = ((bf16[16,256,512]{2,1,0:T(8,128)(2,1)}), bf16[16,256,512]{2,1,0:T(8,128)(2,1)}, u32[]{:S(2)}, u32[]{:S(2)}) async-start(bf16[16,256,512]{2,1,0:T(8,128)(2,1)} %stack.17), calls=%async_computation | async-start | bytes 8388608 | tf_op jit(solution)/shard_map/all_to_all | solution.py:35
  16.2 0.9 copy-start.8
  16.2 1.0 copy-start.9
  16.3 74.2 %copy-start.3 = (bf16[512,512]{1,0:T(8,128)(2,1)S(1)}, bf16[512,512]{1,0:T(8,128)(2,1)}, u32[]{:S(2)}) copy-start(bf16[512,512]{1,0:T(8,128)(2,1)} %param.18) | copy-start | bytes 1572868
  16.3 482.8 %reduce-scatter.9.cloned.1.call-start = ((), (), s32[]{:S(2)}) async-start(), calls=%async_computation.5 | async-start | bytes 17825792 | tf_op jit(solution)/shard_map/reduce_scatter | solution.py:131
  322.1 1.2 copy-start.2
  322.1 245.5 %reduce-scatter.11.cloned.1.call-start = ((), (), s32[]{:S(2)}) async-start(), calls=%async_computation.6 | async-start | bytes 1114112 | tf_op jit(solution)/shard_map/reduce_scatter | solution.py:134
  325.0 330.2 %all-reduce.3.cloned.1.call-start = ((), (), s32[]{:S(2)}) async-start(), calls=%async_computation.9 | async-start | bytes 1179648 | tf_op jit(solution)/shard_map/psum | solution.py:144
  500.4 1.5 copy-start.4
  501.5 66.2 %copy-start.1 = (bf16[256,512]{1,0:T(8,128)(2,1)S(1)}, bf16[256,512]{1,0:T(8,128)(2,1)}, u32[]{:S(2)}) copy-start(bf16[256,512]{1,0:T(8,128)(2,1)} %param.14) | copy-start | bytes 786436
  567.7 149.9 %reduce-scatter.15.cloned.1.call-start = ((), (), s32[]{:S(2)}) async-start(), calls=%async_computation.8 | async-start | bytes 1114112
  569.4 211.1 %reduce-scatter.13.cloned.1.call-start = ((), (), s32[]{:S(2)}) async-start(), calls=%async_computation.7 | async-start | bytes 1114112
Sparse Core Ops, SparseCore 0:
  322.3 176.8 reduce-scatter.8
  501.5 66.0 reduce-scatter.10
  570.4 84.7 all-reduce.2
  658.1 59.4 reduce-scatter.14
  720.4 60.1 reduce-scatter.12
